TPU v7x, 1024 devices: a whole 4x8x16 slice. The times are simulated.
1024 devices in a mesh: group: 8 (over y), expert: 32 (over z, core), rep: 4 (over x).
Axes of the slice: x: 4, y: 8, z: 16, core: 2. Of those that a mesh axis runs over, the one named last changes fastest.
Arguments:
- tokens: bfloat16 [2048, 4096], P(('group', 'expert')), may hold values from -6 to 6
- cotangent: bfloat16 [2048, 4096], P(('group', 'expert')), may hold values from -6 to 6
- router: bfloat16 [4096, 128], P(None, 'group'), may hold values from -0.09375 to 0.09375
- w_gate: bfloat16 [256, 4096, 512], P(('group', 'expert'), None, 'rep'), may hold values from -0.09375 to 0.09375
- w_up: bfloat16 [256, 4096, 512], P(('group', 'expert'), None, 'rep'), may hold values from -0.09375 to 0.09375
- w_down: bfloat16 [256, 512, 4096], P(('group', 'expert'), 'rep'), may hold values from -0.1875 to 0.1875
- group_picks: int32 [8, 32, 64, 2], P('group', 'expert'), may hold values from -1 to 15, as said below
Outputs:
- layer_out: bfloat16 [2048, 4096], P(('group', 'expert'), 'rep')
- input_grad: bfloat16 [2048, 4096], P(('group', 'expert'), 'rep')
Inputs may be any that keep to these rules, and one draw needn't show every extreme that they name: group_picks[g, c, t] holds two different in-group experts that column token t of column c names in group g, or -1 twice where the token names none there. Every token names exactly 4 groups, and each group is named by exactly 32 tokens of every column. In one group and column an expert is named by at most 8 tokens; in every column some experts of every group are named by exactly 8.
All inputs are finite; a program needn't handle non-finite values.
Results may differ from a plain program's by a relative error of at most 0.015.
Values may be sent and summed in bfloat16 or wider, within the bound.
A program may use at most 32 MiB of HBM per device.

v0:
```python
import jax
import jax.numpy as jnp
from jax import lax
from jax.sharding import PartitionSpec as P

route_scale = 2.5


def slot_table(pick_list, local_count, slot_cap):
    expert_ids = jnp.arange(local_count, dtype=jnp.int32)
    onehot = jnp.sum((pick_list[:, :, None] == expert_ids[None, None, :]).astype(jnp.int32), axis=1)
    prior_value = jnp.cumsum(onehot, axis=0) - onehot
    places = jnp.arange(slot_cap, dtype=jnp.int32)
    select = (onehot.T[:, None, :] == 1) & (prior_value.T[:, None, :] == places[None, :, None])
    return (onehot, select)


def on_device(tokens, cotangent, router, w_gate, w_up, w_down, group_picks):
    tok_dev, model_width = tokens.shape
    rep_count = lax.axis_size("rep")
    owner_count = lax.axis_size("expert")
    local_count = router.shape[1]
    halves = owner_count // local_count
    slot_cap = 4 * tok_dev // max(local_count // 4, 1)
    quarter = model_width // rep_count
    largest_score = lax.Precision.HIGHEST
    contract = (((1,), (1,)), ((), ()))
    column_rows, column_grads = (
        lax.all_gather(tokens, "group", axis=0, tiled=True),
        lax.all_gather(cotangent, "group", axis=0, tiled=True),
    )
    onehot, select = slot_table(group_picks[0, 0], local_count, slot_cap)
    select_b = select.astype(jnp.bfloat16)

    def to_slots(column):
        placed = jnp.einsum("ekt,td->ekd", select_b, column)
        return jnp.repeat(placed, halves, axis=0)

    owner_rows, owner_grads = (
        lax.all_to_all(to_slots(column_rows), "expert", split_axis=0, concat_axis=0, tiled=True),
        lax.all_to_all(to_slots(column_grads), "expert", split_axis=0, concat_axis=0, tiled=True),
    )
    expert_scores = jax.nn.sigmoid(jnp.dot(column_rows, router, preferred_element_type=jnp.float32))
    sources = owner_rows.shape[0]
    flat_rows = owner_rows.reshape(-1, model_width)
    gate_value = jnp.dot(flat_rows, w_gate[0], preferred_element_type=jnp.float32)
    up_value = jnp.dot(flat_rows, w_up[0], preferred_element_type=jnp.float32)
    gate_sig = jax.nn.sigmoid(gate_value)
    gate_act = gate_value * gate_sig
    hidden = (gate_act * up_value).astype(jnp.bfloat16)
    out_part = jnp.dot(hidden, w_down[0], preferred_element_type=jnp.float32).reshape(
        sources, slot_cap, model_width
    )
    out_sum = lax.psum_scatter(
        out_part.astype(jnp.bfloat16), "rep", scatter_dimension=2, tiled=True
    )
    flat_grads = owner_grads.reshape(-1, model_width)
    grad_hidden = lax.dot_general(
        flat_grads, w_down[0], contract, preferred_element_type=jnp.float32
    )
    dot_part = jnp.sum(grad_hidden * hidden.astype(jnp.float32), axis=1)
    grad_gate = (grad_hidden * up_value * gate_sig * (1.0 + gate_value * (1.0 - gate_sig))).astype(
        jnp.bfloat16
    )
    grad_up = (grad_hidden * gate_act).astype(jnp.bfloat16)
    joined_grads = jnp.concatenate([grad_gate, grad_up], axis=1)
    joined_weights = jnp.concatenate([w_gate[0], w_up[0]], axis=1)
    grad_part = lax.dot_general(
        joined_grads, joined_weights, contract, preferred_element_type=jnp.float32
    )
    grad_part = grad_part.reshape(sources, slot_cap, model_width)
    dot_rep = jnp.broadcast_to(
        dot_part.reshape(sources, slot_cap, 1), (sources, slot_cap, rep_count)
    )
    grad_back, dot_sum = (
        lax.psum_scatter(
            grad_part.astype(jnp.bfloat16), "rep", scatter_dimension=2, tiled=True
        ).astype(jnp.float32),
        lax.psum_scatter(
            dot_rep.astype(jnp.bfloat16), "rep", scatter_dimension=2, tiled=True
        ).astype(jnp.float32),
    )
    back_out, back_grad, back_dot = (
        lax.all_to_all(out_sum, "expert", split_axis=0, concat_axis=0, tiled=True),
        lax.all_to_all(
            grad_back.astype(jnp.bfloat16), "expert", split_axis=0, concat_axis=0, tiled=True
        ),
        lax.all_to_all(
            dot_sum.astype(jnp.bfloat16), "expert", split_axis=0, concat_axis=0, tiled=True
        ),
    )

    def join_halves(arrived):
        return jnp.sum(
            arrived.astype(jnp.float32).reshape(local_count, halves, slot_cap, arrived.shape[-1]),
            axis=1,
        )

    expert_out = join_halves(back_out).reshape(local_count * slot_cap, quarter)
    expert_grad = join_halves(back_grad).reshape(local_count * slot_cap, quarter)
    expert_dot = join_halves(back_dot)[:, :, 0]
    select_f = select.astype(jnp.float32)
    weighted = (select_f * expert_scores.T[:, None, :]).reshape(local_count * slot_cap, -1)
    mixed_out = jnp.dot(weighted.T, expert_out, precision=largest_score)
    grad_mix = jnp.dot(weighted.T, expert_grad, precision=largest_score)
    pick_dot = jnp.einsum("ekt,ek->te", select_f, expert_dot, precision=largest_score)
    chosen = onehot.astype(jnp.float32)
    gate_slope = expert_scores * (1.0 - expert_scores) * chosen
    router_token_rows = lax.dynamic_slice_in_dim(
        router, lax.axis_index("rep") * quarter, quarter, 0
    ).astype(jnp.float32)
    grad_mix = grad_mix + jnp.dot(
        gate_slope * pick_dot, router_token_rows.T, precision=largest_score
    )
    gate_grad = jnp.dot(gate_slope, router_token_rows.T, precision=largest_score)
    gate_total = jnp.sum(expert_scores * chosen, axis=1)
    dot_total = jnp.sum(expert_scores * chosen * pick_dot, axis=1)
    mix_sum, grad_sum, slope_sum, gate_weight_total, dotted = (
        lax.psum_scatter(mixed_out, "group", scatter_dimension=0, tiled=True),
        lax.psum_scatter(grad_mix, "group", scatter_dimension=0, tiled=True),
        lax.psum_scatter(gate_grad, "group", scatter_dimension=0, tiled=True),
        lax.psum_scatter(gate_total, "group", scatter_dimension=0, tiled=True),
        lax.psum_scatter(dot_total, "group", scatter_dimension=0, tiled=True),
    )
    factor = route_scale / gate_weight_total
    layer_out = (mix_sum * factor[:, None]).astype(jnp.bfloat16)
    input_grad = (
        grad_sum * factor[:, None] - slope_sum * (factor * dotted / gate_weight_total)[:, None]
    ).astype(jnp.bfloat16)
    return (layer_out, input_grad)


def solution(mesh):
    return jax.shard_map(
        on_device,
        mesh=mesh,
        in_specs=(
            P(("group", "expert"), None),
            P(("group", "expert"), None),
            P(None, "group"),
            P(("group", "expert"), None, "rep"),
            P(("group", "expert"), None, "rep"),
            P(("group", "expert"), "rep", None),
            P("group", "expert", None, None),
        ),
        out_specs=(P(("group", "expert"), "rep"), P(("group", "expert"), "rep")),
        check_vma=False,
    )
```

profile of v0, /device:TPU:8, one launch (start us, length us, event | category | flops | bytes accessed | tf_op | source)
XLA Modules:
  0.0 509.1 jit_solution(6954780083556472916)
XLA Ops:
  8.0 0.8 convert_reduce_fusion.2
  8.8 0.1 copy.47
  8.9 0.1 reduce_window_sum.11
  9.0 0.1 copy.49
  9.0 35.4 %all_gather.6 = bf16[64,4096]{1,0:T(8,128)(2,1)S(1)} all-gather(bf16[8,4096]{1,0:T(8,128)(2,1)} %param.7), channel_id=1, replica_groups=mesh['group'=8,'expert'=32,'rep'=4] {'group'}, dimensions={0}, use_global_device_ids=true | all-gather | bytes 589824 | tf_op jit(solution)/shard_map/all_gather | solution.py:29
  44.5 0.8 copy-done.1
  45.2 0.4 fusion.18
  45.7 1.6 broadcast_in_dim.6
  47.3 10.3 %all-to-all-start = ((bf16[32,8,4096]{2,1,0:T(8,128)(2,1)}), bf16[32,8,4096]{2,1,0:T(8,128)(2,1)S(1)}, u32[]{:S(2)}, u32[]{:S(2)}) async-start(bf16[32,8,4096]{2,1,0:T(8,128)(2,1)} %bitcast.69), calls=%async_computation | async-start | bytes 4194304 | tf_op jit(solution)/shard_map/all_to_all | solution.py:40
  57.5 25.4 %all_gather.7 = bf16[64,4096]{1,0:T(8,128)(2,1)S(1)} all-gather(bf16[8,4096]{1,0:T(8,128)(2,1)S(1)} %copy-done.8), channel_id=1, replica_groups=mesh['group'=8,'expert'=32,'rep'=4] {'group'}, dimensions={0}, use_global_device_ids=true | all-gather | bytes 589824 | tf_op jit(solution)/shard_map/all_gather | solution.py:30
  83.0 1.4 fusion.16
  84.4 72.4 %all-to-all-done = bf16[32,8,4096]{2,1,0:T(8,128)(2,1)S(1)} async-done(((bf16[32,8,4096]{2,1,0:T(8,128)(2,1)}), bf16[32,8,4096]{2,1,0:T(8,128)(2,1)S(1)}, u32[]{:S(2)}, u32[]{:S(2)}) %all-to-all-start) | async-done | bytes 2097184 | tf_op jit(solution)/shard_map/all_to_all | solution.py:40
  156.8 2.8 broadcast_in_dim.7
  159.5 4.8 all-to-all-start.2
  164.4 2.0 fusion.6
  166.4 0.7 fusion.8
  167.1 98.6 %all-to-all-done.2 = bf16[32,8,4096]{2,1,0:T(8,128)(2,1)} async-done(((bf16[32,8,4096]{2,1,0:T(8,128)(2,1)}), bf16[32,8,4096]{2,1,0:T(8,128)(2,1)}, u32[]{:S(2)}, u32[]{:S(2)}) %all-to-all-start.2) | async-done | bytes 2097184 | tf_op jit(solution)/shard_map/all_to_all | solution.py:41
  265.7 2.9 multiply_reduce_fusion
  268.7 2.0 convolution_convert_fusion
  270.8 2.0 fusion
  272.9 1.3 dynamic-slice.2
  274.2 0.1 convert_element_type.61
  274.3 0.1 copy.57
  274.4 10.6 %all-reduce.1 = bf16[32,8,4]{0,1,2:T(8,128)(2,1)S(1)} all-reduce(bf16[32,8,4]{0,1,2:T(8,128)(2,1)S(1)} %broadcast_in_dim.8), channel_id=6, replica_groups=mesh['group'=8,'expert'=32,'rep'=4] {'rep'}, use_global_device_ids=true, to_apply=%region_10.11.clone | all-reduce | flops 1024 | bytes 4096
  285.0 0.7 constant_dynamic-slice_fusion
  285.7 0.1 copy.58
  285.8 15.4 %all_to_all.25 = bf16[32,8,1]{1,2,0:T(2,128)(2,1)S(1)} all-to-all(bf16[32,8,1]{1,2,0:T(2,128)(2,1)S(1)} %copy.58), channel_id=1, replica_groups=mesh['group'=8,'expert'=32,'rep'=4] {'expert'}, dimensions={0} | all-to-all | bytes 1024 | tf_op jit(solution)/shard_map/all_to_all | solution.py:88
  301.1 0.4 reduce-scatter.6.cloned.1.call-done
  301.5 13.2 %all-to-all-start.1 = ((bf16[32,8,1024]{2,1,0:T(8,128)(2,1)}), bf16[32,8,1024]{2,1,0:T(8,128)(2,1)S(1)}, u32[]{:S(2)}, u32[]{:S(2)}) async-start(bf16[32,8,1024]{2,1,0:T(8,128)(2,1)} %reduce-scatter.6.cloned.1.call-done), calls=%async_computation.2 | async-start | bytes 1048576 | tf_op jit(solution)/shard_map/all_to_all | solution.py:84
  314.7 30.8 %reduce-scatter.10.cloned.1.call-done = bf16[32,8,1024]{2,1,0:T(8,128)(2,1)} async-done(((bf16[32,8,4096]{2,1,0:T(8,128)(2,1)}), bf16[32,8,1024]{2,1,0:T(8,128)(2,1)}) %reduce-scatter.10.cloned.1.call-update) | async-done | bytes 524304 | tf_op jit(solution)/shard_map/reduce_scatter | solution.py:76
  345.6 2.9 all-to-all-done.1
  348.5 10.4 %all-to-all-start.3 = ((bf16[32,8,1024]{2,1,0:T(8,128)(2,1)}), bf16[32,8,1024]{2,1,0:T(8,128)(2,1)S(1)}, u32[]{:S(2)}, u32[]{:S(2)}) async-start(bf16[32,8,1024]{2,1,0:T(8,128)(2,1)} %reduce-scatter.10.cloned.1.call-done), calls=%async_computation.6 | async-start | bytes 1048576 | tf_op jit(solution)/shard_map/all_to_all | solution.py:85
  359.0 0.2 fusion.31
  359.2 0.3 multiply_reduce_fusion.1
  359.5 1.0 fusion.38
  360.5 0.0 reduce-scatter.8.cloned.1.call-start
  360.6 0.1 convert_reduce_fusion.1
  360.7 1.4 convolution_bitcast_fusion.1
  362.2 0.3 fusion.40
  362.5 30.2 %all-to-all-done.3 = bf16[32,8,1024]{2,1,0:T(8,128)(2,1)S(1)} async-done(((bf16[32,8,1024]{2,1,0:T(8,128)(2,1)}), bf16[32,8,1024]{2,1,0:T(8,128)(2,1)S(1)}, u32[]{:S(2)}, u32[]{:S(2)}) %all-to-all-start.3) | async-done | bytes 524320 | tf_op jit(solution)/shard_map/all_to_all | solution.py:85
  392.6 0.1 convert_reduce_fusion
  392.7 1.4 fusion.10
  394.2 1.3 dynamic-slice
  396.1 15.8 %all-reduce.3 = (f32[64]{0:T(128)S(1)}, f32[64]{0:T(128)S(1)}) all-reduce(f32[64]{0:T(128)S(1)} %get-tuple-element.3, f32[64]{0:T(128)S(1)} %get-tuple-element.2), channel_id=4, replica_groups=mesh['group'=8,'expert'=32,'rep'=4] {'group'}, use_global_device_ids=true, to_apply=%region_6.7.clone | all-reduce | flops 128 | bytes 1024
  411.9 0.1 fusion.47
  412.0 41.2 %reduce-scatter.8.cloned.1.call-done = f32[8,1024]{1,0:T(8,128)} async-done(((f32[64,1024]{1,0:T(8,128)}), f32[8,1024]{1,0:T(8,128)}) %reduce-scatter.8.cloned.1.call-update) | async-done | bytes 32784 | tf_op jit(solution)/shard_map/reduce_scatter | solution.py:119
  453.1 46.9 %reduce-scatter.12.cloned.1.call-done = f32[8,1024]{1,0:T(8,128)} async-done(((f32[64,1024]{1,0:T(8,128)}), f32[8,1024]{1,0:T(8,128)}) %reduce-scatter.12.cloned.1.call-update) | async-done | bytes 32784 | tf_op jit(solution)/shard_map/reduce_scatter | solution.py:120
  500.0 1.5 subtract_convert_fusion
  (33 shorter events, 0.4 us)
Async XLA Ops:
  8.0 257.7 %copy-start = (bf16[1,128,4096]{2,1,0:T(8,128)(2,1)S(1)}, bf16[1,128,4096]{2,1,0:T(8,128)(2,1)}, u32[]{:S(2)}) copy-start(bf16[1,128,4096]{2,1,0:T(8,128)(2,1)} %param.12) | copy-start | bytes 3145732
  44.4 0.8 copy-start.1
  47.3 10.3 %copy-start.8 = (bf16[8,4096]{1,0:T(8,128)(2,1)S(1)}, bf16[8,4096]{1,0:T(8,128)(2,1)}, u32[]{:S(2)}) copy-start(bf16[8,4096]{1,0:T(8,128)(2,1)} %param.8) | copy-start | bytes 196612
  47.3 109.5 %all-to-all-start = ((bf16[32,8,4096]{2,1,0:T(8,128)(2,1)}), bf16[32,8,4096]{2,1,0:T(8,128)(2,1)S(1)}, u32[]{:S(2)}, u32[]{:S(2)}) async-start(bf16[32,8,4096]{2,1,0:T(8,128)(2,1)} %bitcast.69), calls=%async_computation | async-start | bytes 4194304 | tf_op jit(solution)/shard_map/all_to_all | solution.py:40
  159.5 106.2 %all-to-all-start.2 = ((bf16[32,8,4096]{2,1,0:T(8,128)(2,1)}), bf16[32,8,4096]{2,1,0:T(8,128)(2,1)}, u32[]{:S(2)}, u32[]{:S(2)}) async-start(bf16[32,8,4096]{2,1,0:T(8,128)(2,1)} %bitcast.68), calls=%async_computation.4 | async-start | bytes 4194304 | tf_op jit(solution)/shard_map/all_to_all | solution.py:41
  164.3 137.2 %reduce-scatter.6.cloned.1.call-start = ((), (), s32[]{:S(2)}) async-start(), calls=%async_computation.10 | async-start | bytes 2621440 | tf_op jit(solution)/shard_map/reduce_scatter | solution.py:54
  164.4 2.0 copy-start.4
  268.7 2.1 copy-start.3
  268.7 2.1 copy-start.5
  268.7 2.2 copy-start.7
  270.7 74.8 %reduce-scatter.10.cloned.1.call-start = ((), (), s32[]{:S(2)}) async-start(), calls=%async_computation.12 | async-start | bytes 2621440 | tf_op jit(solution)/shard_map/reduce_scatter | solution.py:76
  272.9 86.3 %copy-start.2 = (bf16[64,4096]{1,0:T(8,128)(2,1)S(1)}, bf16[64,4096]{1,0:T(8,128)(2,1)}, u32[]{:S(2)}) copy-start(bf16[64,4096]{1,0:T(8,128)(2,1)} %copy-done.1) | copy-start | bytes 1572868
  272.9 86.3 %copy-start.6 = (bf16[4096,16]{0,1:T(8,128)(2,1)S(1)}, bf16[4096,16]{0,1:T(8,128)(2,1)}, u32[]{:S(2)}) copy-start(bf16[4096,16]{0,1:T(8,128)(2,1)} %param.9) | copy-start | bytes 393220
  301.5 47.0 %all-to-all-start.1 = ((bf16[32,8,1024]{2,1,0:T(8,128)(2,1)}), bf16[32,8,1024]{2,1,0:T(8,128)(2,1)S(1)}, u32[]{:S(2)}, u32[]{:S(2)}) async-start(bf16[32,8,1024]{2,1,0:T(8,128)(2,1)} %reduce-scatter.6.cloned.1.call-done), calls=%async_computation.2 | async-start | bytes 1048576 | tf_op jit(solution)/shard_map/all_to_all | solution.py:84
  348.5 44.2 %all-to-all-start.3 = ((bf16[32,8,1024]{2,1,0:T(8,128)(2,1)}), bf16[32,8,1024]{2,1,0:T(8,128)(2,1)S(1)}, u32[]{:S(2)}, u32[]{:S(2)}) async-start(bf16[32,8,1024]{2,1,0:T(8,128)(2,1)} %reduce-scatter.10.cloned.1.call-done), calls=%async_computation.6 | async-start | bytes 1048576 | tf_op jit(solution)/shard_map/all_to_all | solution.py:85
  358.9 53.1 %reduce-scatter.14.cloned.1.call-start = ((), (), s32[]{:S(2)}) async-start(), calls=%async_computation.14 | async-start | bytes 294912 | tf_op jit(solution)/shard_map/reduce_scatter | solution.py:121
  360.5 92.6 %reduce-scatter.8.cloned.1.call-start = ((), (), s32[]{:S(2)}) async-start(), calls=%async_computation.11 | async-start | bytes 294912 | tf_op jit(solution)/shard_map/reduce_scatter | solution.py:119
  362.1 137.9 %reduce-scatter.12.cloned.1.call-start = ((), (), s32[]{:S(2)}) async-start(), calls=%async_computation.13 | async-start | bytes 294912 | tf_op jit(solution)/shard_map/reduce_scatter | solution.py:120
Sparse Core Ops, SparseCore 0:
  270.9 30.5 reduce-scatter.5
  305.3 40.2 reduce-scatter.9
Sparse Core Ops, SparseCore 1:
  362.7 43.4 reduce-scatter.13
  409.4 43.7 reduce-scatter.7
  456.4 43.6 reduce-scatter.11
where the time goes:
time: 510 us; the launch traced here: 509 us
  waiting for transfers between devices  324 us (64%)
  blocking collectives  103 us (20%)
  starting transfers between devices  38.8 us (8%)
  between operations  16.5 us (3%)
  matrix products  16.1 us (3%)
  local copies, waits for them, and re-layouts  8.85 us (2%)
    all_to_all x1, waiting for transfers between devices, on_device(): lax.all_to_all(to_slots(column_grads), 'expert', split_axis=0, concat_axi...  98.6 us
    all_to_all x1, waiting for transfers between devices, on_device(): lax.all_to_all(to_slots(column_rows), 'expert', split_axis=0, concat_axis...  72.4 us
    reduce_scatter x1, waiting for transfers between devices, on_device(): lax.psum_scatter(grad_mix, 'group', scatter_dimension=0, tiled=True)  46.9 us
    reduce_scatter x1, waiting for transfers between devices, on_device(): lax.psum_scatter(mixed_out, 'group', scatter_dimension=0, tiled=True)  41.2 us
    all_gather x1, blocking collectives, on_device(): lax.all_gather(tokens, 'group', axis=0, tiled=True)  35.4 us
    reduce_scatter x1, waiting for transfers between devices, on_device(): lax.psum_scatter(grad_part.astype(jnp.bfloat16), 'rep', scatter_dimension...  30.8 us
    all_to_all x1, waiting for transfers between devices, on_device(): lax.all_to_all(grad_back.astype(jnp.bfloat16), 'expert', split_axis=0, co...  30.2 us
    unnamed x2, blocking collectives  26.4 us
  transfers between devices with their start and end apart: 9, of which 8 were waited for; matrix products, arithmetic and copies ran while one was open for 3% of the time, Pallas kernels for 0%

commit v1 on v0

v1 whole, which is shorter than its diff:
```python
import functools

import jax
import jax.numpy as jnp
from jax import lax
from jax.experimental import pallas as pl
from jax.experimental.pallas import tpu as pltpu
from jax.sharding import PartitionSpec as P

MESH = pl.DeviceIdType.MESH
F32 = jnp.float32
BF16 = jnp.bfloat16
route_scale = 2.5
NT = (((1,), (1,)), ((), ()))


def rcopy(src, dst, send, recv, device):
    return pltpu.make_async_remote_copy(
        src_ref=src, dst_ref=dst, send_sem=send, recv_sem=recv, device_id=device, device_id_type=MESH
    )


def kernel(
    ny, nz, nx, chunks,
    tok_ref, cot_ref, router_ref, wg_ref, wu_ref, wd_ref, picks_ref,
    out_ref, grad_ref,
    wgu, wd, col, rt, slots, xr, pt, prcv, sa, ra, sb, rb, zs, ret, mg, mgr, st, hs, lg, pd, sel_s, wt,
    w_sem,
    yt_s, yt_r, yr_s, yr_r, ym_s, ym_r, ys_s, ys_r,
    zf_s, zf_r, zr_s, zr_r,
    lg_s, lg_r, pd_s, pd_r,
    xa_s, xa_r, xd_s, xd_r, pc_s, pc_r, pr_s, pr_r, ra_s, ra_r, rb_s, rb_r,
):
    y = lax.axis_index("group")
    e = lax.axis_index("expert")
    x = lax.axis_index("rep")
    z = e // 2
    core = e % 2
    other = 1 - core
    width = tok_ref.shape[1] // nx
    groups = nz // chunks
    half = chunks // 2
    lanes = ny * 16
    right, left = (x + 1) % nx, (x + nx - 1) % nx
    across = (x + 2) % nx

    def at_y(i):
        return {"group": i}

    def at_z(i):
        return {"expert": i * 2 + core}

    def at_x(i):
        return {"rep": i}

    partner = {"expert": z * 2 + other}

    def offset(p):
        g = p // 2
        m = (g + 1) // 2
        sign = 2 * (g % 2) - 1
        return (p % 2) * (-sign * (nz // 2 - m)) + (1 - p % 2) * (sign * m)

    load_gate = pltpu.make_async_copy(wg_ref.at[0], wgu.at[:, 0:128], w_sem.at[0])
    load_up = pltpu.make_async_copy(wu_ref.at[0], wgu.at[:, 128:256], w_sem.at[1])
    load_down = pltpu.make_async_copy(wd_ref.at[0], wd, w_sem.at[2])
    load_gate.start()
    load_up.start()
    load_down.start()

    barrier = pltpu.get_barrier_semaphore()
    for d in range(1, ny):
        pl.semaphore_signal(barrier, inc=1, device_id=at_y((y + d) % ny), device_id_type=MESH)
    for d in range(1, nx):
        pl.semaphore_signal(barrier, inc=1, device_id=at_x((x + d) % nx), device_id_type=MESH)
    pl.semaphore_signal(barrier, inc=1, device_id=partner, device_id_type=MESH)

    def greet(d, carry):
        pl.semaphore_signal(barrier, inc=1, device_id=at_z((z + d) % nz), device_id_type=MESH)
        return carry

    lax.fori_loop(1, nz, greet, 0)
    quarter = pl.ds(pl.multiple_of(x * width, 128), width)
    col[y] = jnp.concatenate(
        [tok_ref[:, quarter].astype(F32), cot_ref[:, quarter].astype(F32)], axis=0
    ).astype(BF16)
    rt[y] = router_ref[:, quarter]
    pl.semaphore_wait(barrier, ny - 1 + nx - 1 + 1 + nz - 1)

    for d in range(1, ny):
        there = (y + d) % ny
        rcopy(col.at[y], col.at[y], yt_s.at[d], yt_r.at[d], at_y(there)).start()
    for d in range(1, ny):
        there = (y + d) % ny
        rcopy(rt.at[y], rt.at[y], yr_s.at[d], yr_r.at[d], at_y(there)).start()

    picks = picks_ref[...]
    tokens_here = ny * 8
    ids = lax.broadcasted_iota(jnp.int32, (nz, tokens_here), 0)
    onehot = ((picks[0:1, :] == ids) | (picks[1:2, :] == ids)).astype(F32).astype(BF16)
    t_row = lax.broadcasted_iota(jnp.int32, (tokens_here, lanes), 0)
    q_col = lax.broadcasted_iota(jnp.int32, (tokens_here, lanes), 1)
    t_col = (q_col // 16) * 8 + q_col % 8
    spread = (t_row == t_col).astype(F32).astype(BF16)
    before = (t_row < t_col).astype(F32).astype(BF16)
    onehot_q = jnp.dot(onehot, spread, preferred_element_type=F32)
    prior = jnp.dot(onehot, before, preferred_element_type=F32)
    shape3 = (nz, 16, lanes)
    row = lax.broadcasted_iota(jnp.int32, shape3, 1)
    lane = lax.broadcasted_iota(jnp.int32, shape3, 2)
    same_kind = (row // 8) == ((lane // 8) % 2)
    slot = (row % 8).astype(F32)
    picked = jnp.where(
        same_kind & (jnp.broadcast_to(prior[:, None, :], shape3) == slot),
        jnp.broadcast_to(onehot_q[:, None, :], shape3),
        0.0,
    )
    sel_s[...] = picked

    for d in range(1, ny):
        rcopy(col.at[y], col.at[(y + ny - d) % ny], yt_s.at[d], yt_r.at[d], at_y(y)).wait_recv()
    column = col[...].reshape(lanes, width)
    slots[...] = (
        jnp.dot(picked.reshape(nz * 16, lanes).astype(BF16), column, preferred_element_type=F32)
        .astype(BF16)
        .reshape(nz, 16, width)
    )

    def z_forward(p):
        there = (z - offset(p) + nz) % nz
        return rcopy(slots.at[there], xr.at[x, p, core], zf_s.at[p], zf_r.at[p], at_z(there))

    def z_send(p, carry):
        z_forward(p).start()
        return carry

    lax.fori_loop(1, nz, z_send, 0)
    xr[x, 0, core] = slots[z]

    logits = lax.dot_general(rt[y], column, NT, preferred_element_type=F32)
    lg[x] = logits
    for d in range(1, nx):
        rcopy(lg.at[x], lg.at[x], lg_s.at[d], lg_r.at[d], at_x((x + d) % nx)).start()

    def part(g):
        return pl.ds(g * chunks, chunks)

    def first(g):
        return pl.ds(g * chunks, half)

    def second(g):
        return pl.ds(g * chunks + half, half)

    def to_side(q, g, side, device):
        block = xr.at[q, part(g), core]
        return rcopy(block, block, xa_s.at[g, side], xa_r.at[g, side], device)

    def onward(q, places, g, side, device):
        block = xr.at[q, places, core]
        return rcopy(block, block, xd_s.at[g, side], xd_r.at[g, side], device)

    def to_partner(q, g):
        block = xr.at[q, part(g), core]
        return rcopy(block, block, pc_s.at[g, q], pc_r.at[g, q], partner)

    def from_partner(q, g):
        block = xr.at[q, part(g), other]
        return rcopy(block, block, pc_s.at[g, q], pc_r.at[g, q], partner)

    def parts_to_partner(g):
        return rcopy(pt.at[:, part(g), other], prcv.at[:, part(g)], pr_s.at[g], pr_r.at[g], partner)

    def pair_sum(q, places):
        return pt[q, places, core].astype(F32) + prcv[q, places].astype(F32)

    def sum_across(places, g, side, device):
        return rcopy(sa.at[places], ra.at[places], ra_s.at[g, side], ra_r.at[g, side], device)

    def sum_side(g, side, device):
        return rcopy(sb.at[side, part(g)], rb.at[side, part(g)], rb_s.at[g, side], rb_r.at[g, side], device)

    def z_back(p):
        there = (z + offset(p) + nz) % nz
        return rcopy(zs.at[p], ret.at[z], zr_s.at[p], zr_r.at[p], at_z(there))

    def stage_arrive(g):
        def wait_one(p, carry):
            z_forward(p).wait_recv()
            return carry

        lax.fori_loop(jnp.maximum(g * chunks, 1), (g + 1) * chunks, wait_one, 0)
        to_side(x, g, 0, at_x(right)).start()
        to_side(x, g, 1, at_x(left)).start()
        to_partner(x, g).start()

    def stage_sides(g):
        to_side(left, g, 0, at_x(right)).wait_recv()
        onward(left, first(g), g, 0, at_x(right)).start()
        to_partner(left, g).start()
        to_side(right, g, 1, at_x(left)).wait_recv()
        onward(right, second(g), g, 1, at_x(left)).start()
        to_partner(right, g).start()

    def stage_across(g):
        onward(across, first(g), g, 0, at_x(right)).wait_recv()
        onward(across, second(g), g, 1, at_x(left)).wait_recv()
        to_partner(across, g).start()

    def stage_compute(g):
        for q in range(nx):
            from_partner(q, g).wait_recv()
        rows = chunks * 2
        gate_up = jnp.zeros((rows * 16, 256), F32)
        grad_hidden = jnp.zeros((rows * 16, 128), F32)
        for q in range(nx):
            block = xr[q, part(g)].reshape(rows * 16, width)
            depth = slice(q * width, (q + 1) * width)
            gate_up = gate_up + jnp.dot(block, wgu[depth, :], preferred_element_type=F32)
            grad_hidden = grad_hidden + lax.dot_general(
                block, wd[:, depth], NT, preferred_element_type=F32
            )
        gate_up = gate_up.reshape(rows, 16, 256)[:, 0:8, :].reshape(rows * 8, 256)
        grad_hidden = grad_hidden.reshape(rows, 16, 128)[:, 8:16, :].reshape(rows * 8, 128)
        gate, up = gate_up[:, 0:128], gate_up[:, 128:256]
        sig = jax.nn.sigmoid(gate)
        act = gate * sig
        hidden = (act * up).astype(BF16)
        both = jnp.concatenate(
            [grad_hidden * up * sig * (1.0 + gate * (1.0 - sig)), grad_hidden * act], axis=1
        ).astype(BF16)
        for q in range(nx):
            depth = slice(q * width, (q + 1) * width)
            out = jnp.dot(hidden, wd[:, depth], preferred_element_type=F32)
            grad = lax.dot_general(both, wgu[depth, :], NT, preferred_element_type=F32)
            joined = jnp.concatenate(
                [out.reshape(rows, 8, width), grad.reshape(rows, 8, width)], axis=1
            ).astype(BF16)
            pt[q, part(g)] = joined.reshape(chunks, 2, 16, width)
        parts_to_partner(g).start()

    def stage_pair(g):
        parts_to_partner(g).wait_recv()
        sa[part(g)] = pair_sum(across, part(g)).astype(BF16)
        sum_across(first(g), g, 0, at_x(right)).start()
        sum_across(second(g), g, 1, at_x(left)).start()

    def stage_add(g):
        sum_across(first(g), g, 0, at_x(right)).wait_recv()
        sum_across(second(g), g, 1, at_x(left)).wait_recv()
        sb[0, first(g)] = (pair_sum(right, first(g)) + ra[first(g)].astype(F32)).astype(BF16)
        sb[0, second(g)] = pair_sum(right, second(g)).astype(BF16)
        sum_side(g, 0, at_x(right)).start()
        sb[1, first(g)] = pair_sum(left, first(g)).astype(BF16)
        sb[1, second(g)] = (pair_sum(left, second(g)) + ra[second(g)].astype(F32)).astype(BF16)
        sum_side(g, 1, at_x(left)).start()

    def stage_return(g):
        sum_side(g, 0, at_x(right)).wait_recv()
        sum_side(g, 1, at_x(left)).wait_recv()
        zs[part(g)] = (
            pair_sum(x, part(g)) + rb[0, part(g)].astype(F32) + rb[1, part(g)].astype(F32)
        ).astype(BF16)

        def send_one(p, carry):
            z_back(p).start()
            return carry

        lax.fori_loop(jnp.maximum(g * chunks, 1), (g + 1) * chunks, send_one, 0)

    load_gate.wait()
    load_up.wait()
    load_down.wait()

    stages = (
        stage_arrive, stage_sides, stage_across, stage_compute, stage_pair, stage_add, stage_return
    )

    def step(it, carry):
        for lag in range(len(stages) - 1, -1, -1):
            g = it - lag

            @pl.when((g >= 0) & (g < groups))
            def _(stage=stages[lag], g=g):
                stage(g)

        return carry

    lax.fori_loop(0, groups + len(stages) - 1, step, 0)

    for d in range(1, nx):
        rcopy(lg.at[x], lg.at[(x + nx - d) % nx], lg_s.at[d], lg_r.at[d], at_x(x)).wait_recv()
    score = jax.nn.sigmoid((lg[0] + lg[1]) + (lg[2] + lg[3]))
    lane2 = lax.broadcasted_iota(jnp.int32, (nz, lanes), 1)
    token_lane = (lane2 // 8) % 2 == 0
    score = jnp.where(token_lane, score, pltpu.roll(score, 8, 1))
    weighted = sel_s[...] * jnp.broadcast_to(score[:, None, :], shape3)
    weighted = jnp.transpose(weighted.reshape(nz * 16, lanes))
    high = weighted.astype(BF16)
    wt[0] = high
    wt[1] = (weighted - high.astype(F32)).astype(BF16)

    ret[z] = zs[0]

    def wait_back(p, carry):
        there = (z - offset(p) + nz) % nz
        rcopy(zs.at[p], ret.at[there], zr_s.at[p], zr_r.at[p], at_z(z)).wait_recv()
        return carry

    lax.fori_loop(1, nz, wait_back, 0)
    back = ret[...].reshape(nz * 16, width)
    cross = lax.dot_general(back, col[...].reshape(lanes, width), NT, preferred_element_type=F32)
    cross = cross.reshape(shape3)[:, 0:8, :] * sel_s[:, 8:16, :]
    pd[x] = jnp.sum(cross, axis=1)
    for d in range(1, nx):
        rcopy(pd.at[x], pd.at[x], pd_s.at[d], pd_r.at[d], at_x((x + d) % nx)).start()
    mixed = jnp.dot(wt[0], back, preferred_element_type=F32) + jnp.dot(
        wt[1], back, preferred_element_type=F32
    )
    mg[...] = mixed.astype(BF16).reshape(ny, 16, width)
    for d in range(1, ny):
        there = (y + d) % ny
        rcopy(mg.at[there], mgr.at[y], ym_s.at[d], ym_r.at[d], at_y(there)).start()
    mgr[y] = mg[y]
    for d in range(1, nx):
        rcopy(pd.at[x], pd.at[(x + nx - d) % nx], pd_s.at[d], pd_r.at[d], at_x(x)).wait_recv()
    table = jnp.where(token_lane, score * onehot_q, (pd[0] + pd[1]) + (pd[2] + pd[3]))
    table = jnp.concatenate([table, jnp.zeros((128 - nz, lanes), F32)], axis=0)
    st[...] = jnp.transpose(table).reshape(ny, 16, 128)
    for d in range(1, ny):
        there = (y + d) % ny
        rcopy(st.at[there], hs.at[y], ys_s.at[d], ys_r.at[d], at_y(there)).start()
    hs[y] = st[y]

    for d in range(1, ny):
        there = (y + ny - d) % ny
        rcopy(rt.at[there], rt.at[there], yr_s.at[d], yr_r.at[d], at_y(y)).wait_recv()
        rcopy(mg.at[there], mgr.at[there], ym_s.at[d], ym_r.at[d], at_y(y)).wait_recv()
        rcopy(st.at[there], hs.at[there], ys_s.at[d], ys_r.at[d], at_y(y)).wait_recv()
    total = mgr[0].astype(F32)
    terms = hs[0]
    for g in range(1, ny):
        total = total + mgr[g].astype(F32)
        terms = terms + pltpu.roll(hs[g], g * nz, 1)
    s, dots = terms[0:8], terms[8:16]
    slope = s * (1.0 - s)
    dot_slope = slope * dots
    slope_high = slope.astype(BF16).astype(F32)
    dot_high = dot_slope.astype(BF16).astype(F32)
    factors = jnp.concatenate(
        [slope_high, slope - slope_high, dot_high, dot_slope - dot_high], axis=0
    ).astype(BF16)
    experts = ny * nz
    by_router = jnp.dot(
        factors[:, 0:experts], rt[...].reshape(experts, width), preferred_element_type=F32
    )
    slope_sum = by_router[0:8] + by_router[8:16]
    grad_sum = total[8:16] + (by_router[16:24] + by_router[24:32])
    gate_sum = jnp.sum(s, axis=1, keepdims=True)
    dot_sum = jnp.sum(s * dots, axis=1, keepdims=True)
    factor = route_scale / gate_sum
    out_ref[...] = (total[0:8] * factor).astype(BF16)
    grad_ref[...] = (grad_sum * factor - slope_sum * (factor * dot_sum / gate_sum)).astype(BF16)

    for d in range(1, ny):
        rcopy(col.at[y], col.at[y], yt_s.at[d], yt_r.at[d], at_y(y)).wait_send()
        rcopy(rt.at[y], rt.at[y], yr_s.at[d], yr_r.at[d], at_y(y)).wait_send()
        rcopy(mg.at[y], mgr.at[y], ym_s.at[d], ym_r.at[d], at_y(y)).wait_send()
        rcopy(st.at[y], hs.at[y], ys_s.at[d], ys_r.at[d], at_y(y)).wait_send()
    for d in range(1, nx):
        rcopy(lg.at[x], lg.at[x], lg_s.at[d], lg_r.at[d], at_x(x)).wait_send()
        rcopy(pd.at[x], pd.at[x], pd_s.at[d], pd_r.at[d], at_x(x)).wait_send()

    def sent_z(p, carry):
        z_forward(p).wait_send()
        z_back(p).wait_send()
        return carry

    lax.fori_loop(1, nz, sent_z, 0)

    def sent_group(g, carry):
        to_side(x, g, 0, at_x(right)).wait_send()
        to_side(x, g, 1, at_x(left)).wait_send()
        onward(left, first(g), g, 0, at_x(right)).wait_send()
        onward(right, second(g), g, 1, at_x(left)).wait_send()
        for q in range(nx):
            to_partner(q, g).wait_send()
        parts_to_partner(g).wait_send()
        sum_across(first(g), g, 0, at_x(right)).wait_send()
        sum_across(second(g), g, 1, at_x(left)).wait_send()
        sum_side(g, 0, at_x(right)).wait_send()
        sum_side(g, 1, at_x(left)).wait_send()
        return carry

    lax.fori_loop(0, groups, sent_group, 0)


def on_device(chunks, tokens, cotangent, router, w_gate, w_up, w_down, group_picks):
    ny = lax.axis_size("group")
    nz = lax.axis_size("expert") // 2
    nx = lax.axis_size("rep")
    width = tokens.shape[1] // nx
    groups = nz // chunks
    lanes = ny * 16
    dma = pltpu.SemaphoreType.DMA
    vmem = pl.BlockSpec(memory_space=pltpu.VMEM)
    hbm = pl.BlockSpec(memory_space=pl.ANY)
    result = jax.ShapeDtypeStruct((tokens.shape[0], width), BF16)
    return pl.pallas_call(
        functools.partial(kernel, ny, nz, nx, chunks),
        out_shape=(result, result),
        in_specs=[vmem, vmem, vmem, hbm, hbm, hbm, vmem],
        out_specs=(vmem, vmem),
        scratch_shapes=[
            pltpu.VMEM((nx * width, 256), BF16),
            pltpu.VMEM((128, nx * width), BF16),
            pltpu.VMEM((ny, 16, width), BF16),
            pltpu.VMEM((ny, nz, width), BF16),
            pltpu.VMEM((nz, 16, width), BF16),
            pltpu.VMEM((nx, nz, 2, 16, width), BF16),
            pltpu.VMEM((nx, nz, 2, 16, width), BF16),
            pltpu.VMEM((nx, nz, 16, width), BF16),
            pltpu.VMEM((nz, 16, width), BF16),
            pltpu.VMEM((nz, 16, width), BF16),
            pltpu.VMEM((2, nz, 16, width), BF16),
            pltpu.VMEM((2, nz, 16, width), BF16),
            pltpu.VMEM((nz, 16, width), BF16),
            pltpu.VMEM((nz, 16, width), BF16),
            pltpu.VMEM((ny, 16, width), BF16),
            pltpu.VMEM((ny, 16, width), BF16),
            pltpu.VMEM((ny, 16, 128), F32),
            pltpu.VMEM((ny, 16, 128), F32),
            pltpu.VMEM((nx, nz, lanes), F32),
            pltpu.VMEM((nx, nz, lanes), F32),
            pltpu.VMEM((nz, 16, lanes), F32),
            pltpu.VMEM((2, lanes, nz * 16), BF16),
            dma((3,)),
        ]
        + [dma((ny,))] * 8
        + [dma((nz,))] * 4
        + [dma((nx,))] * 4
        + [dma((groups, 2))] * 4
        + [dma((groups, nx))] * 2
        + [dma((groups,))] * 2
        + [dma((groups, 2))] * 4,
        compiler_params=pltpu.CompilerParams(
            collective_id=0, has_side_effects=True, vmem_limit_bytes=56 * 1024 * 1024
        ),
        cost_estimate=pl.CostEstimate(
            flops=3 * 1024 * 1024 * 1024, bytes_accessed=4 * 1024 * 1024, transcendentals=32768
        ),
    )(tokens, cotangent, router.T, w_gate, w_up, w_down, group_picks[0, 0].T)


def solution(mesh):
    return jax.shard_map(
        functools.partial(on_device, 4),
        mesh=mesh,
        in_specs=(
            P(("group", "expert"), None),
            P(("group", "expert"), None),
            P(None, "group"),
            P(("group", "expert"), None, "rep"),
            P(("group", "expert"), None, "rep"),
            P(("group", "expert"), "rep", None),
            P("group", "expert", None, None),
        ),
        out_specs=(P(("group", "expert"), "rep"), P(("group", "expert"), "rep")),
        check_vma=False,
    )
```

time: 510 us -> 119 us (0.23)
  the two profiles are of different devices: /device:TPU:8 before, /device:TPU:2 now
where the time goes in v1:
time: 119 us
  Pallas kernels  116 us (97%)
  local copies, waits for them, and re-layouts  1.94 us (2%)
    pallas_call x1, Pallas kernels, on_device(): pl.pallas_call(functools.partial(kernel, ny, nz, nx, chunks), out_shape=(...  116 us

profile of v1, /device:TPU:2, one launch (start us, length us, event | category | flops | bytes accessed | tf_op | source)
XLA Modules:
  0.0 119.1 jit_solution(8907790388827903474)
XLA Ops:
  0.6 116.5 %shard_map.86 = (bf16[8,1024]{1,0:T(8,128)(2,1)}, bf16[8,1024]{1,0:T(8,128)(2,1)}) custom-call(bf16[8,4096]{1,0:T(8,128)(2,1)} %tok_ref.1, bf16[8,4096]{1,0:T(8,128)(2,1)} %cot_ref.1, bf16[16,4096]{1,0:T(8,128)(2,1)} %bitcast.4, bf16[1,4096,128]{2,1,0:T(8,128)(2,1)} %wg_ref.1, bf16[1,4096,128]{2,1,0:T(8,128)(2,1)} %wu_ref.1, bf16[1,128,4096]{2,1,0:T(8,128)(2,1)} %wd_ref.1, ...), custom_call_target="tpu_custom_call" | custom-call | flops 3221225472 | bytes 4194304 | tf_op jit(solution)/shard_map/pallas_call | solution.py:408
  117.1 0.0 copy-start
  117.1 1.3 %copy.11 = bf16[8,1024]{1,0:T(8,128)(2,1)} copy(bf16[8,1024]{1,0:T(8,128)(2,1)} %get-tuple-element.4) | data formatting | bytes 32768
  118.5 0.0 copy-done
  118.5 0.6 copy.12
Async XLA Ops:
  117.1 1.3 %copy-start = (bf16[8,1024]{1,0:T(8,128)(2,1)S(1)}, bf16[8,1024]{1,0:T(8,128)(2,1)}, u32[]{:S(2)}) copy-start(bf16[8,1024]{1,0:T(8,128)(2,1)} %get-tuple-element.5) | copy-start | bytes 49156

commit v2 on v1

--- a/solution.py
+++ b/solution.py
@@ -21,15 +21,15 @@
 
 
 def kernel(
-    ny, nz, nx, chunks,
+    ny, nz, nx, chunks, window,
     tok_ref, cot_ref, router_ref, wg_ref, wu_ref, wd_ref, picks_ref,
     out_ref, grad_ref,
-    wgu, wd, col, rt, slots, xr, pt, prcv, sa, ra, sb, rb, zs, ret, mg, mgr, st, hs, lg, pd, sel_s, wt,
+    wgu, wd, wgu_t, wd_t, col, rt, slots, xr, pt, prcv, sb, rb, zs, ret, mg, mgr, st, hs, lg, pd, sel_s, wt,
     w_sem,
     yt_s, yt_r, yr_s, yr_r, ym_s, ym_r, ys_s, ys_r,
     zf_s, zf_r, zr_s, zr_r,
     lg_s, lg_r, pd_s, pd_r,
-    xa_s, xa_r, xd_s, xd_r, pc_s, pc_r, pr_s, pr_r, ra_s, ra_r, rb_s, rb_r,
+    xa_s, xa_r, pc_s, pc_r, pr_s, pr_r, rb_s, rb_r,
 ):
     y = lax.axis_index("group")
     e = lax.axis_index("expert")
@@ -39,21 +39,18 @@
     other = 1 - core
     width = tok_ref.shape[1] // nx
     groups = nz // chunks
-    half = chunks // 2
     lanes = ny * 16
-    right, left = (x + 1) % nx, (x + nx - 1) % nx
-    across = (x + 2) % nx
 
     def at_y(i):
-        return {"group": i}
+        return (i, e, x)
 
     def at_z(i):
-        return {"expert": i * 2 + core}
+        return (y, i * 2 + core, x)
 
     def at_x(i):
-        return {"rep": i}
-
-    partner = {"expert": z * 2 + other}
+        return (y, e, i)
+
+    partner = (y, z * 2 + other, x)
 
     def offset(p):
         g = p // 2
@@ -90,9 +87,6 @@
     for d in range(1, ny):
         there = (y + d) % ny
         rcopy(col.at[y], col.at[y], yt_s.at[d], yt_r.at[d], at_y(there)).start()
-    for d in range(1, ny):
-        there = (y + d) % ny
-        rcopy(rt.at[y], rt.at[y], yr_s.at[d], yr_r.at[d], at_y(there)).start()
 
     picks = picks_ref[...]
     tokens_here = ny * 8
@@ -117,6 +111,14 @@
     )
     sel_s[...] = picked
 
+    load_gate.wait()
+    load_up.wait()
+    load_down.wait()
+    for q in range(nx):
+        depth = slice(q * width, (q + 1) * width)
+        wgu_t[:, depth] = jnp.transpose(wgu[depth, :])
+        wd_t[depth, :] = jnp.transpose(wd[:, depth])
+
     for d in range(1, ny):
         rcopy(col.at[y], col.at[(y + ny - d) % ny], yt_s.at[d], yt_r.at[d], at_y(y)).wait_recv()
     column = col[...].reshape(lanes, width)
@@ -134,30 +136,29 @@
         z_forward(p).start()
         return carry
 
-    lax.fori_loop(1, nz, z_send, 0)
+    def z_send_group(g):
+        lax.fori_loop(jnp.maximum(g * chunks, 1), (g + 1) * chunks, z_send, 0)
+
+    lax.fori_loop(1, min(window, groups) * chunks, z_send, 0)
     xr[x, 0, core] = slots[z]
 
     logits = lax.dot_general(rt[y], column, NT, preferred_element_type=F32)
     lg[x] = logits
+    for d in range(1, ny):
+        rcopy(rt.at[y], rt.at[y], yr_s.at[d], yr_r.at[d], at_y((y + d) % ny)).start()
     for d in range(1, nx):
         rcopy(lg.at[x], lg.at[x], lg_s.at[d], lg_r.at[d], at_x((x + d) % nx)).start()
 
     def part(g):
         return pl.ds(g * chunks, chunks)
 
-    def first(g):
-        return pl.ds(g * chunks, half)
-
-    def second(g):
-        return pl.ds(g * chunks + half, half)
-
-    def to_side(q, g, side, device):
-        block = xr.at[q, part(g), core]
-        return rcopy(block, block, xa_s.at[g, side], xa_r.at[g, side], device)
-
-    def onward(q, places, g, side, device):
-        block = xr.at[q, places, core]
-        return rcopy(block, block, xd_s.at[g, side], xd_r.at[g, side], device)
+    def to_plane(d, g):
+        block = xr.at[x, part(g), core]
+        return rcopy(block, block, xa_s.at[g, d], xa_r.at[g, d], at_x((x + d) % nx))
+
+    def from_plane(d, g):
+        block = xr.at[(x + nx - d) % nx, part(g), core]
+        return rcopy(block, block, xa_s.at[g, d], xa_r.at[g, d], at_x(x))
 
     def to_partner(q, g):
         block = xr.at[q, part(g), core]
@@ -173,11 +174,9 @@
     def pair_sum(q, places):
         return pt[q, places, core].astype(F32) + prcv[q, places].astype(F32)
 
-    def sum_across(places, g, side, device):
-        return rcopy(sa.at[places], ra.at[places], ra_s.at[g, side], ra_r.at[g, side], device)
-
-    def sum_side(g, side, device):
-        return rcopy(sb.at[side, part(g)], rb.at[side, part(g)], rb_s.at[g, side], rb_r.at[g, side], device)
+    def sum_to(d, g):
+        there = (x + d) % nx
+        return rcopy(sb.at[d, part(g)], rb.at[d, part(g)], rb_s.at[g, d], rb_r.at[g, d], at_x(there))
 
     def z_back(p):
         there = (z + offset(p) + nz) % nz
@@ -189,22 +188,19 @@
             return carry
 
         lax.fori_loop(jnp.maximum(g * chunks, 1), (g + 1) * chunks, wait_one, 0)
-        to_side(x, g, 0, at_x(right)).start()
-        to_side(x, g, 1, at_x(left)).start()
+
+        @pl.when(g + window < groups)
+        def _():
+            z_send_group(g + window)
+
+        for d in (2, 1, 3):
+            to_plane(d, g).start()
         to_partner(x, g).start()
 
-    def stage_sides(g):
-        to_side(left, g, 0, at_x(right)).wait_recv()
-        onward(left, first(g), g, 0, at_x(right)).start()
-        to_partner(left, g).start()
-        to_side(right, g, 1, at_x(left)).wait_recv()
-        onward(right, second(g), g, 1, at_x(left)).start()
-        to_partner(right, g).start()
-
-    def stage_across(g):
-        onward(across, first(g), g, 0, at_x(right)).wait_recv()
-        onward(across, second(g), g, 1, at_x(left)).wait_recv()
-        to_partner(across, g).start()
+    def stage_planes(g):
+        for d in (1, 3, 2):
+            from_plane(d, g).wait_recv()
+            to_partner((x + nx - d) % nx, g).start()
 
     def stage_compute(g):
         for q in range(nx):
@@ -216,9 +212,7 @@
             block = xr[q, part(g)].reshape(rows * 16, width)
             depth = slice(q * width, (q + 1) * width)
             gate_up = gate_up + jnp.dot(block, wgu[depth, :], preferred_element_type=F32)
-            grad_hidden = grad_hidden + lax.dot_general(
-                block, wd[:, depth], NT, preferred_element_type=F32
-            )
+            grad_hidden = grad_hidden + jnp.dot(block, wd_t[depth, :], preferred_element_type=F32)
         gate_up = gate_up.reshape(rows, 16, 256)[:, 0:8, :].reshape(rows * 8, 256)
         grad_hidden = grad_hidden.reshape(rows, 16, 128)[:, 8:16, :].reshape(rows * 8, 128)
         gate, up = gate_up[:, 0:128], gate_up[:, 128:256]
@@ -231,7 +225,7 @@
         for q in range(nx):
             depth = slice(q * width, (q + 1) * width)
             out = jnp.dot(hidden, wd[:, depth], preferred_element_type=F32)
-            grad = lax.dot_general(both, wgu[depth, :], NT, preferred_element_type=F32)
+            grad = jnp.dot(both, wgu_t[:, depth], preferred_element_type=F32)
             joined = jnp.concatenate(
                 [out.reshape(rows, 8, width), grad.reshape(rows, 8, width)], axis=1
             ).astype(BF16)
@@ -240,26 +234,16 @@
 
     def stage_pair(g):
         parts_to_partner(g).wait_recv()
-        sa[part(g)] = pair_sum(across, part(g)).astype(BF16)
-        sum_across(first(g), g, 0, at_x(right)).start()
-        sum_across(second(g), g, 1, at_x(left)).start()
-
-    def stage_add(g):
-        sum_across(first(g), g, 0, at_x(right)).wait_recv()
-        sum_across(second(g), g, 1, at_x(left)).wait_recv()
-        sb[0, first(g)] = (pair_sum(right, first(g)) + ra[first(g)].astype(F32)).astype(BF16)
-        sb[0, second(g)] = pair_sum(right, second(g)).astype(BF16)
-        sum_side(g, 0, at_x(right)).start()
-        sb[1, first(g)] = pair_sum(left, first(g)).astype(BF16)
-        sb[1, second(g)] = (pair_sum(left, second(g)) + ra[second(g)].astype(F32)).astype(BF16)
-        sum_side(g, 1, at_x(left)).start()
+        for d in (2, 1, 3):
+            sb[d, part(g)] = pair_sum((x + d) % nx, part(g)).astype(BF16)
+            sum_to(d, g).start()
 
     def stage_return(g):
-        sum_side(g, 0, at_x(right)).wait_recv()
-        sum_side(g, 1, at_x(left)).wait_recv()
-        zs[part(g)] = (
-            pair_sum(x, part(g)) + rb[0, part(g)].astype(F32) + rb[1, part(g)].astype(F32)
-        ).astype(BF16)
+        total = pair_sum(x, part(g))
+        for d in range(1, nx):
+            sum_to(d, g).wait_recv()
+            total = total + rb[d, part(g)].astype(F32)
+        zs[part(g)] = total.astype(BF16)
 
         def send_one(p, carry):
             z_back(p).start()
@@ -267,25 +251,21 @@
 
         lax.fori_loop(jnp.maximum(g * chunks, 1), (g + 1) * chunks, send_one, 0)
 
-    load_gate.wait()
-    load_up.wait()
-    load_down.wait()
-
     stages = (
-        stage_arrive, stage_sides, stage_across, stage_compute, stage_pair, stage_add, stage_return
+        (stage_arrive, 0), (stage_return, 5), (stage_compute, 2), (stage_pair, 3), (stage_planes, 1),
     )
 
     def step(it, carry):
-        for lag in range(len(stages) - 1, -1, -1):
+        for stage, lag in stages:
             g = it - lag
 
             @pl.when((g >= 0) & (g < groups))
-            def _(stage=stages[lag], g=g):
+            def _(stage=stage, g=g):
                 stage(g)
 
         return carry
 
-    lax.fori_loop(0, groups + len(stages) - 1, step, 0)
+    lax.fori_loop(0, groups + 5, step, 0)
 
     for d in range(1, nx):
         rcopy(lg.at[x], lg.at[(x + nx - d) % nx], lg_s.at[d], lg_r.at[d], at_x(x)).wait_recv()
@@ -378,23 +358,18 @@
     lax.fori_loop(1, nz, sent_z, 0)
 
     def sent_group(g, carry):
-        to_side(x, g, 0, at_x(right)).wait_send()
-        to_side(x, g, 1, at_x(left)).wait_send()
-        onward(left, first(g), g, 0, at_x(right)).wait_send()
-        onward(right, second(g), g, 1, at_x(left)).wait_send()
+        for d in range(1, nx):
+            to_plane(d, g).wait_send()
+            sum_to(d, g).wait_send()
         for q in range(nx):
             to_partner(q, g).wait_send()
         parts_to_partner(g).wait_send()
-        sum_across(first(g), g, 0, at_x(right)).wait_send()
-        sum_across(second(g), g, 1, at_x(left)).wait_send()
-        sum_side(g, 0, at_x(right)).wait_send()
-        sum_side(g, 1, at_x(left)).wait_send()
         return carry
 
     lax.fori_loop(0, groups, sent_group, 0)
 
 
-def on_device(chunks, tokens, cotangent, router, w_gate, w_up, w_down, group_picks):
+def on_device(chunks, window, tokens, cotangent, router, w_gate, w_up, w_down, group_picks):
     ny = lax.axis_size("group")
     nz = lax.axis_size("expert") // 2
     nx = lax.axis_size("rep")
@@ -406,23 +381,23 @@
     hbm = pl.BlockSpec(memory_space=pl.ANY)
     result = jax.ShapeDtypeStruct((tokens.shape[0], width), BF16)
     return pl.pallas_call(
-        functools.partial(kernel, ny, nz, nx, chunks),
+        functools.partial(kernel, ny, nz, nx, chunks, window),
         out_shape=(result, result),
         in_specs=[vmem, vmem, vmem, hbm, hbm, hbm, vmem],
         out_specs=(vmem, vmem),
         scratch_shapes=[
             pltpu.VMEM((nx * width, 256), BF16),
             pltpu.VMEM((128, nx * width), BF16),
+            pltpu.VMEM((256, nx * width), BF16),
+            pltpu.VMEM((nx * width, 128), BF16),
             pltpu.VMEM((ny, 16, width), BF16),
             pltpu.VMEM((ny, nz, width), BF16),
             pltpu.VMEM((nz, 16, width), BF16),
             pltpu.VMEM((nx, nz, 2, 16, width), BF16),
             pltpu.VMEM((nx, nz, 2, 16, width), BF16),
             pltpu.VMEM((nx, nz, 16, width), BF16),
-            pltpu.VMEM((nz, 16, width), BF16),
-            pltpu.VMEM((nz, 16, width), BF16),
-            pltpu.VMEM((2, nz, 16, width), BF16),
-            pltpu.VMEM((2, nz, 16, width), BF16),
+            pltpu.VMEM((nx, nz, 16, width), BF16),
+            pltpu.VMEM((nx, nz, 16, width), BF16),
             pltpu.VMEM((nz, 16, width), BF16),
             pltpu.VMEM((nz, 16, width), BF16),
             pltpu.VMEM((ny, 16, width), BF16),
@@ -438,10 +413,9 @@
         + [dma((ny,))] * 8
         + [dma((nz,))] * 4
         + [dma((nx,))] * 4
-        + [dma((groups, 2))] * 4
-        + [dma((groups, nx))] * 2
+        + [dma((groups, nx))] * 4
         + [dma((groups,))] * 2
-        + [dma((groups, 2))] * 4,
+        + [dma((groups, nx))] * 2,
         compiler_params=pltpu.CompilerParams(
             collective_id=0, has_side_effects=True, vmem_limit_bytes=56 * 1024 * 1024
         ),
@@ -453,7 +427,7 @@
 
 def solution(mesh):
     return jax.shard_map(
-        functools.partial(on_device, 4),
+        functools.partial(on_device, 2, 8),
         mesh=mesh,
         in_specs=(
             P(("group", "expert"), None),

time: 119 us -> 115 us (0.966)
  the two profiles are of different devices: /device:TPU:2 before, /device:TPU:64 now
where the time goes in v2:
time: 115 us
  Pallas kernels  112 us (97%)
  local copies, waits for them, and re-layouts  1.94 us (2%)
    pallas_call x1, Pallas kernels, on_device(): pl.pallas_call(functools.partial(kernel, ny, nz, nx, chunks, window), out...  112 us

profile of v2, /device:TPU:64, one launch (start us, length us, event | category | flops | bytes accessed | tf_op | source)
XLA Modules:
  0.0 114.8 jit_solution(7264225972678615429)
XLA Ops:
  0.6 112.2 %shard_map.86 = (bf16[8,1024]{1,0:T(8,128)(2,1)}, bf16[8,1024]{1,0:T(8,128)(2,1)}) custom-call(bf16[8,4096]{1,0:T(8,128)(2,1)} %tok_ref.1, bf16[8,4096]{1,0:T(8,128)(2,1)} %cot_ref.1, bf16[16,4096]{1,0:T(8,128)(2,1)} %bitcast.4, bf16[1,4096,128]{2,1,0:T(8,128)(2,1)} %wg_ref.1, bf16[1,4096,128]{2,1,0:T(8,128)(2,1)} %wu_ref.1, bf16[1,128,4096]{2,1,0:T(8,128)(2,1)} %wd_ref.1, ...), custom_call_target="tpu_custom_call" | custom-call | flops 3221225472 | bytes 4194304 | tf_op jit(solution)/shard_map/pallas_call | solution.py:383
  112.9 0.0 copy-start
  112.9 1.3 %copy.11 = bf16[8,1024]{1,0:T(8,128)(2,1)} copy(bf16[8,1024]{1,0:T(8,128)(2,1)} %get-tuple-element.4) | data formatting | bytes 32768
  114.2 0.0 copy-done
  114.2 0.6 copy.12
Async XLA Ops:
  112.9 1.3 %copy-start = (bf16[8,1024]{1,0:T(8,128)(2,1)S(1)}, bf16[8,1024]{1,0:T(8,128)(2,1)}, u32[]{:S(2)}) copy-start(bf16[8,1024]{1,0:T(8,128)(2,1)} %get-tuple-element.5) | copy-start | bytes 49156

commit v3 on v2

--- a/solution.py
+++ b/solution.py
@@ -252,7 +252,7 @@
         lax.fori_loop(jnp.maximum(g * chunks, 1), (g + 1) * chunks, send_one, 0)
 
     stages = (
-        (stage_arrive, 0), (stage_return, 5), (stage_compute, 2), (stage_pair, 3), (stage_planes, 1),
+        (stage_arrive, 0), (stage_return, 4), (stage_compute, 2), (stage_planes, 1), (stage_pair, 2),
     )
 
     def step(it, carry):
@@ -265,7 +265,7 @@
 
         return carry
 
-    lax.fori_loop(0, groups + 5, step, 0)
+    lax.fori_loop(0, groups + 4, step, 0)
 
     for d in range(1, nx):
         rcopy(lg.at[x], lg.at[(x + nx - d) % nx], lg_s.at[d], lg_r.at[d], at_x(x)).wait_recv()

time: 115 us -> 115 us (level)
  the two profiles are of different devices: /device:TPU:64 before, /device:TPU:66 now
where the time goes in v3:
time: 115 us
  Pallas kernels  112 us (97%)
  local copies, waits for them, and re-layouts  1.94 us (2%)
    pallas_call x1, Pallas kernels, on_device(): pl.pallas_call(functools.partial(kernel, ny, nz, nx, chunks, window), out...  112 us

profile of v3, /device:TPU:66, one launch (start us, length us, event | category | flops | bytes accessed | tf_op | source)
XLA Modules:
  0.0 115.0 jit_solution(893205029574574052)
XLA Ops:
  0.6 112.4 %shard_map.86 = (bf16[8,1024]{1,0:T(8,128)(2,1)}, bf16[8,1024]{1,0:T(8,128)(2,1)}) custom-call(bf16[8,4096]{1,0:T(8,128)(2,1)} %tok_ref.1, bf16[8,4096]{1,0:T(8,128)(2,1)} %cot_ref.1, bf16[16,4096]{1,0:T(8,128)(2,1)} %bitcast.4, bf16[1,4096,128]{2,1,0:T(8,128)(2,1)} %wg_ref.1, bf16[1,4096,128]{2,1,0:T(8,128)(2,1)} %wu_ref.1, bf16[1,128,4096]{2,1,0:T(8,128)(2,1)} %wd_ref.1, ...), custom_call_target="tpu_custom_call" | custom-call | flops 3221225472 | bytes 4194304 | tf_op jit(solution)/shard_map/pallas_call | solution.py:383
  113.0 0.0 copy-start
  113.0 1.3 %copy.11 = bf16[8,1024]{1,0:T(8,128)(2,1)} copy(bf16[8,1024]{1,0:T(8,128)(2,1)} %get-tuple-element.4) | data formatting | bytes 32768
  114.4 0.0 copy-done
  114.4 0.6 copy.12
Async XLA Ops:
  113.0 1.3 %copy-start = (bf16[8,1024]{1,0:T(8,128)(2,1)S(1)}, bf16[8,1024]{1,0:T(8,128)(2,1)}, u32[]{:S(2)}) copy-start(bf16[8,1024]{1,0:T(8,128)(2,1)} %get-tuple-element.5) | copy-start | bytes 49156
